TPU v7x, 32 devices: a whole 2x2x4 slice. The times are simulated.
32 devices in a mesh: cell: 2 (over core), grp: 16 (over z, y, x).
Axes of the slice: x: 2, y: 2, z: 4, core: 2. Of those that a mesh axis runs over, the one named last changes fastest.
Arguments:
- v_free: float32 [3, 262144], P(None, 'grp'), may hold values from -6 to 6
- inv_mass: float32 [262144], P('grp'), may hold values from 0.2 to 5
- pairs: int32 [2, 1024, 128], P(None, ('cell', 'grp')), may hold values from 0 to 20479, as said below
- angles: float32 [2, 1024, 128], P(None, ('cell', 'grp')), may hold values from -3.140625 to 3.140625
- bias: float32 [1024, 128], P(('cell', 'grp')), may hold values from -6 to 6
- friction: float32 [1024, 128], P(('cell', 'grp')), may hold values from 0.2 to 1
- counts: int32 [1024], P(('cell', 'grp')), may hold values from 16 to 128, as said below
Outputs:
- velocity: float32 [3, 262144], P(None, 'grp')
- impulses: float32 [3, 1024, 128], P(None, ('cell', 'grp'))
Inputs may be any that keep to these rules, and one draw needn't show every extreme that they name: A spatial cell's window of bodies holds the last 2048 bodies of the previous cell (positions 0 to 2047), the cell's own 16384 bodies (positions 2048 to 18431) and the first 2048 bodies of the next cell (the remaining positions). pairs[0] is always one of the cell's own bodies; pairs[1] is another own body or a rim body of a neighbouring cell. No slot of the first cell names the previous rim and no slot of the last cell names the next rim. `counts`: the first block of each 32 blocks is full.
All inputs are finite; a program needn't handle non-finite values.
Results may differ from a plain program's by a relative error of at most 0.0001.
Values sent between devices are 32-bit elements; how exact they have to be, the bound alone decides.
A program may use at most 128 MiB of HBM per device.

v0:
```python
import functools

import jax
import jax.numpy as jnp
from jax import lax
from jax.experimental import pallas as pl
from jax.experimental.pallas import tpu as pltpu
from jax.sharding import PartitionSpec as P

RIM = 2048
ITERS = 3
LANES = 128

relax_factor = 0.6
tangent_floor = 0.05


def split_terms(value):
    high = value.astype(jnp.bfloat16)
    low = (value - high.astype(jnp.float32)).astype(jnp.bfloat16)
    return high, low


def kernel(
    cells,
    counts_ref, v_ref, mass_ref, pairs_ref, angles_ref, bias_ref, friction_ref,
    vel_out, imp_out,
    hot1, hot2, row1, row2, active,
    h1_ref, h2_ref, l1_ref, l2_ref,
    vb, vfree_all, mass_all, rel, partial, force_ref, acc_outer, acc_inner,
    edge_out, edge_in, outer, outer_in, inner, inner_in, bound_out, bound_in,
    edge_send, edge_recv, outer_send, outer_recv, inner_send, inner_recv, bound_send, bound_recv,
):
    rows = v_ref.shape[1]
    rim = RIM // LANES
    half = rows // 2
    deep = half + rim
    mid = half - rim
    tiles = pairs_ref.shape[1] // 8
    core = lax.axis_index("cell")
    cell = lax.axis_index("grp")
    has_prev = cell > 0
    has_next = cell < cells - 1
    present = (has_prev, has_next)
    steps = (-1, 1)

    barrier = pltpu.get_barrier_semaphore()
    pl.semaphore_signal(barrier, inc=1, device_id={"cell": 1 - core}, device_id_type=pl.DeviceIdType.MESH)
    for side in range(2):
        @pl.when(present[side])
        def _():
            pl.semaphore_signal(
                barrier, inc=1, device_id={"grp": cell + steps[side]}, device_id_type=pl.DeviceIdType.MESH
            )

    edge_out[0, 0:3] = v_ref[:, 0:rim]
    edge_out[0, 3] = mass_ref[0:rim]
    edge_out[1, 0:3] = v_ref[:, rows - rim:rows]
    edge_out[1, 3] = mass_ref[rows - rim:rows]
    for side in range(2):
        @pl.when(jnp.logical_not(present[side]))
        def _():
            edge_in[side] = jnp.zeros(edge_in.shape[1:], jnp.float32)
            for sweep in range(ITERS):
                bound_in[sweep, side] = jnp.zeros(bound_in.shape[2:], jnp.float32)

    between = jnp.logical_and(has_prev, has_next)

    @pl.when(between)
    def _():
        pl.semaphore_wait(barrier, 3)

    @pl.when(jnp.logical_not(between))
    def _():
        pl.semaphore_wait(barrier, 2)

    def edge_copy(side):
        return pltpu.make_async_remote_copy(
            src_ref=edge_out.at[side], dst_ref=edge_in.at[1 - side],
            send_sem=edge_send.at[side], recv_sem=edge_recv.at[1 - side],
            device_id={"grp": cell + steps[side]}, device_id_type=pl.DeviceIdType.MESH,
        )

    def outer_copy(sweep):
        return pltpu.make_async_remote_copy(
            src_ref=outer.at[sweep], dst_ref=outer_in.at[sweep],
            send_sem=outer_send.at[sweep], recv_sem=outer_recv.at[sweep],
            device_id={"cell": 1 - core}, device_id_type=pl.DeviceIdType.MESH,
        )

    def inner_copy(sweep):
        return pltpu.make_async_remote_copy(
            src_ref=inner.at[sweep], dst_ref=inner_in.at[sweep],
            send_sem=inner_send.at[sweep], recv_sem=inner_recv.at[sweep],
            device_id={"cell": 1 - core}, device_id_type=pl.DeviceIdType.MESH,
        )

    def bound_copy(sweep, side):
        size = rim if sweep == ITERS - 1 else 2 * rim
        return pltpu.make_async_remote_copy(
            src_ref=bound_out.at[sweep, side, :, pl.ds(0, size)],
            dst_ref=bound_in.at[sweep, 1 - side, :, pl.ds(0, size)],
            send_sem=bound_send.at[sweep, side], recv_sem=bound_recv.at[sweep, 1 - side],
            device_id={"grp": cell + steps[side]}, device_id_type=pl.DeviceIdType.MESH,
        )

    for side in range(2):
        @pl.when(present[side])
        def _():
            edge_copy(side).start()

    def place(position):
        own = position - RIM
        r = own >> 7
        lane = own & (LANES - 1)
        upper = r >= half
        h = jnp.where(upper, jnp.where(r >= rows - rim, r - (rows - rim), r - (half - rim)), r)
        l = jnp.where(upper, LANES, 0) + lane
        before = position < RIM
        after = own >= rows * LANES
        h = jnp.where(before, half + (position >> 7), jnp.where(after, half + r - rows, h))
        l = jnp.where(before, lane, jnp.where(after, LANES + lane, l))
        return h, l

    h1_ref[...], l1_ref[...] = place(pairs_ref[0])
    h2_ref[...], l2_ref[...] = place(pairs_ref[1])

    slot = lax.broadcasted_iota(jnp.int32, (1, LANES), 1)
    for r in range(pairs_ref.shape[1]):
        active[r:r + 1, :] = jnp.where(slot < counts_ref[r], 1.0, 0.0)

    def pair_row(tile, u):
        return jnp.concatenate([tile[2 * u:2 * u + 1], tile[2 * u + 1:2 * u + 2]], axis=1)

    wide = 2 * LANES
    iota_l = lax.broadcasted_iota(jnp.int32, (wide, wide), 0)
    iota_h = lax.broadcasted_iota(jnp.int32, (half, wide), 0)
    iota_o = lax.broadcasted_iota(jnp.int32, (rim, wide), 0)
    iota_m = lax.broadcasted_iota(jnp.int32, (mid, wide), 0) + rim
    iota_r = lax.broadcasted_iota(jnp.int32, (rim, wide), 0) + half

    sin_p, cos_p = jnp.sin(angles_ref[0]), jnp.cos(angles_ref[0])
    sin_q, cos_q = jnp.sin(angles_ref[1]), jnp.cos(angles_ref[1])
    normal = (sin_p * cos_q, sin_p * sin_q, cos_p)
    first_tan = (cos_p * cos_q, cos_p * sin_q, -sin_p)
    second_tan = (-sin_q, cos_q)

    def fold(block):
        lower = block[..., 0:half, :]
        upper = jnp.concatenate([block[..., rows - rim:rows, :], block[..., half:rows - rim, :]], axis=-2)
        return jnp.concatenate([lower, upper], axis=-1)

    vfree_all[:, 0:half] = fold(v_ref[...])
    mass_all[0:half] = fold(mass_ref[...])

    def tile_at(i):
        return pl.ds(pl.multiple_of(i * 8, 8), 8)

    def store_terms(parts, base):
        count, size = len(parts), parts[0].shape[0]
        for c, part in enumerate(parts):
            for t, term in enumerate(split_terms(part)):
                at = base + (t * count + c) * size
                vb[at:at + size, :] = term

    def picked(g, base, size, c, count, mask):
        a = base + c * size
        b = a + count * size
        block = jnp.where(mask, g[a:a + size] + g[b:b + size], 0.0)
        return jnp.sum(block.reshape(size // 8, 8, wide), axis=0)

    def gather_inner(count, fresh):
        @pl.loop(0, tiles)
        def _(i):
            h1, h2 = h1_ref[tile_at(i), :], h2_ref[tile_at(i), :]
            l1, l2 = l1_ref[tile_at(i), :], l2_ref[tile_at(i), :]
            for u in range(4):
                cut = slice(u * wide, (u + 1) * wide)
                h1_row, h2_row = pair_row(h1, u), pair_row(h2, u)
                if fresh:
                    hot1[i, :, cut] = jnp.where(iota_l == pair_row(l1, u), 1.0, 0.0).astype(jnp.bfloat16)
                    hot2[i, :, cut] = jnp.where(iota_l == pair_row(l2, u), 1.0, 0.0).astype(jnp.bfloat16)
                    row1[i, :, cut] = jnp.where(iota_h == h1_row, 1.0, 0.0).astype(jnp.bfloat16)
                    row2[i, 0:half, cut] = jnp.where(iota_h == h2_row, 1.0, 0.0).astype(jnp.bfloat16)
                    row2[i, half:deep, cut] = jnp.where(iota_r == h2_row, 1.0, 0.0).astype(jnp.bfloat16)
                source = vb[0:2 * count * mid, :]
                g1 = jnp.dot(source, hot1[i, :, cut], preferred_element_type=jnp.float32)
                g2 = jnp.dot(source, hot2[i, :, cut], preferred_element_type=jnp.float32)
                at1, at2 = iota_m == h1_row, iota_m == h2_row
                for c in range(count):
                    first = picked(g1, 0, mid, c, count, at1)
                    second = picked(g2, 0, mid, c, count, at2)
                    partial[i, u, c] = first + second if c == 3 else first - second

    def gather_outer(count):
        base = 2 * count * mid
        own = 2 * count * rim

        @pl.loop(0, tiles)
        def _(i):
            h1, h2 = h1_ref[tile_at(i), :], h2_ref[tile_at(i), :]
            found = [[] for _ in range(count)]
            for u in range(4):
                cut = slice(u * wide, (u + 1) * wide)
                h1_row, h2_row = pair_row(h1, u), pair_row(h2, u)
                g1 = jnp.dot(vb[base:base + own, :], hot1[i, :, cut], preferred_element_type=jnp.float32)
                g2 = jnp.dot(vb[base:base + 2 * own, :], hot2[i, :, cut], preferred_element_type=jnp.float32)
                at1, at2, at_rim = iota_o == h1_row, iota_o == h2_row, iota_r == h2_row
                for c in range(count):
                    first = picked(g1, 0, rim, c, count, at1)
                    second = picked(g2, 0, rim, c, count, at2) + picked(g2, own, rim, c, count, at_rim)
                    both_ends = partial[i, u, c] + (first + second if c == 3 else first - second)
                    line = jnp.sum(both_ends, axis=0, keepdims=True)
                    found[c] += [line[:, 0:LANES], line[:, LANES:wide]]
            for c in range(count):
                rel[c, tile_at(i), :] = jnp.concatenate(found[c], axis=0)

    contract = (((1,), (1,)), ((), ()))

    def force_terms(i):
        pieces = []
        for c in range(3):
            tile = force_ref[c, tile_at(i), :]
            wide_row = jnp.concatenate([tile[s:s + 1] for s in range(8)], axis=1)
            pieces.append(split_terms(jnp.broadcast_to(wide_row, (16, 8 * LANES))))
        return pieces

    def weigh(mask, pieces, sign):
        size = mask.shape[0]
        done = []
        for t in range(2):
            for c in range(3):
                block = mask.reshape(size // 16, 16, 8 * LANES) * (sign * pieces[c][t])[None]
                done.append(block.reshape(size, 8 * LANES))
        return done

    def product(weighed, hot):
        return lax.dot_general(
            jnp.concatenate(weighed, axis=0), hot, contract, preferred_element_type=jnp.float32
        )

    def scatter_outer():
        acc_outer[...] = jnp.zeros(acc_outer.shape, jnp.float32)

        @pl.loop(0, tiles)
        def _(i):
            pieces = force_terms(i)
            mine = weigh(row1[i, 0:rim], pieces, 1)
            theirs = weigh(row2[i, 0:rim], pieces, -1) + weigh(row2[i, half:deep], pieces, -1)
            acc_outer[0:6 * rim, :] += product(mine, hot1[i])
            acc_outer[...] += product(theirs, hot2[i])

    def scatter_inner(begin, end):
        @pl.loop(begin, end)
        def _(i):
            pieces = force_terms(i)
            mine = product(weigh(row1[i, rim:half], pieces, 1), hot1[i])
            theirs = product(weigh(row2[i, rim:half], pieces, -1), hot2[i])
            acc_inner[...] += mine + theirs

    lambdas = [jnp.zeros(bias_ref.shape, jnp.float32)] * 3
    reduced = None
    for sweep in range(ITERS):
        last = sweep == ITERS - 1
        if sweep == 0:
            store_terms([vfree_all[c, rim:half] for c in range(3)] + [mass_all[rim:half]], 0)
            gather_inner(4, True)
            for side in range(2):
                @pl.when(present[side])
                def _():
                    edge_copy(1 - side).wait_recv()
            for side in range(2):
                cut = slice(side * LANES, (side + 1) * LANES)
                vfree_all[:, half:deep, cut] = edge_in[side, 0:3]
                mass_all[half:deep, cut] = edge_in[side, 3]
            base = 8 * mid
            store_terms([vfree_all[c, 0:rim] for c in range(3)] + [mass_all[0:rim]], base)
            store_terms([vfree_all[c, half:deep] for c in range(3)] + [mass_all[half:deep]], base + 8 * rim)
            gather_outer(4)
            reduced = relax_factor / rel[3]
        x, y, z = rel[0], rel[1], rel[2]
        speed_n = normal[0] * x + normal[1] * y + normal[2] * z + bias_ref[...]
        speed_a = first_tan[0] * x + first_tan[1] * y + first_tan[2] * z
        speed_b = second_tan[0] * x + second_tan[1] * y
        trial_n = lambdas[0] - reduced * speed_n
        trial_a = lambdas[1] - reduced * speed_a
        trial_b = lambdas[2] - reduced * speed_b
        normal_imp = jnp.maximum(trial_n, 0.0)
        tan_size = jnp.sqrt(trial_a * trial_a + trial_b * trial_b)
        factor = jnp.minimum(1.0, friction_ref[...] * normal_imp / jnp.maximum(tan_size, tangent_floor))
        live = active[...]
        lambdas = [normal_imp * live, trial_a * factor * live, trial_b * factor * live]
        for c in range(3):
            force = normal[c] * lambdas[0] + first_tan[c] * lambdas[1]
            if c < 2:
                force = force + second_tan[c] * lambdas[2]
            force_ref[c] = force

        scatter_outer()
        for c in range(3):
            for part in range(2):
                a = (6 * part + c) * rim
                b = a + 3 * rim
                outer[sweep, c, part * rim:(part + 1) * rim] = acc_outer[a:a + rim, :] + acc_outer[b:b + rim, :]
        outer_copy(sweep).start()
        acc_inner[...] = jnp.zeros(acc_inner.shape, jnp.float32)
        scatter_inner(0, tiles // 2)
        outer_copy(sweep).wait_recv()
        for side in range(2):
            cut = slice(side * LANES, (side + 1) * LANES)
            bound_out[sweep, side, :, 0:rim] = outer[sweep, :, rim:2 * rim, cut] + outer_in[sweep, :, rim:2 * rim, cut]
            bound_out[sweep, side, :, rim:2 * rim] = outer[sweep, :, 0:rim, cut] + outer_in[sweep, :, 0:rim, cut]
        for side in range(2):
            @pl.when(present[side])
            def _():
                bound_copy(sweep, side).start()
        scatter_inner(tiles // 2, tiles)
        for c in range(3):
            a = c * mid
            b = a + 3 * mid
            inner[sweep, c] = acc_inner[a:a + mid, :] + acc_inner[b:b + mid, :]
        inner_copy(sweep).start()
        inner_copy(sweep).wait_recv()
        speeds = []
        for c in range(3):
            total = inner[sweep, c] + inner_in[sweep, c]
            speeds.append(vfree_all[c, rim:half] + mass_all[rim:half] * total)
        if last:
            for c in range(3):
                vel_out[c, rim:half] = speeds[c][:, 0:LANES]
                vel_out[c, half:rows - rim] = speeds[c][:, LANES:wide]
                imp_out[c] = lambdas[c]
        else:
            store_terms(speeds, 0)
            gather_inner(3, False)
        for side in range(2):
            @pl.when(present[side])
            def _():
                bound_copy(sweep, 1 - side).wait_recv()
        for part in range(1 if last else 2):
            here = slice((1 - part) * rim, (2 - part) * rim)
            there = slice(part * rim, (part + 1) * rim)
            body = slice(0, rim) if part == 0 else slice(half, deep)
            speeds = []
            for c in range(3):
                total = jnp.concatenate(
                    [bound_out[sweep, s, c, here] + bound_in[sweep, s, c, there] for s in range(2)], axis=-1
                )
                speeds.append(vfree_all[c, body] + mass_all[body] * total)
            if last:
                for c in range(3):
                    vel_out[c, 0:rim] = speeds[c][:, 0:LANES]
                    vel_out[c, rows - rim:rows] = speeds[c][:, LANES:wide]
            else:
                store_terms(speeds, 6 * mid + 6 * rim * part)
        if not last:
            gather_outer(3)
    for side in range(2):
        @pl.when(present[side])
        def _():
            edge_copy(side).wait_send()
            for sweep in range(ITERS):
                bound_copy(sweep, side).wait_send()
    for sweep in range(ITERS):
        outer_copy(sweep).wait_send()
        inner_copy(sweep).wait_send()


def on_device(cells, v_free, inv_mass, pairs, angles, bias, friction, counts):
    width = v_free.shape[1]
    blocks, slots = bias.shape
    rows = width // LANES
    rim = RIM // LANES
    half = rows // 2
    deep = half + rim
    mid = half - rim
    tiles = blocks // 8
    wide = 2 * LANES
    f32, bf16, i32 = jnp.float32, jnp.bfloat16, jnp.int32
    vmem = pl.BlockSpec(memory_space=pltpu.VMEM)
    dma = pltpu.SemaphoreType.DMA
    velocity, impulses = pl.pallas_call(
        functools.partial(kernel, cells),
        out_shape=(
            jax.ShapeDtypeStruct((3, rows, LANES), f32),
            jax.ShapeDtypeStruct((3, blocks, slots), f32),
        ),
        in_specs=[pl.BlockSpec(memory_space=pltpu.SMEM)] + [vmem] * 6,
        out_specs=(vmem, vmem),
        scratch_shapes=[
            pltpu.VMEM((tiles, wide, 8 * LANES), bf16),
            pltpu.VMEM((tiles, wide, 8 * LANES), bf16),
            pltpu.VMEM((tiles, half, 8 * LANES), bf16),
            pltpu.VMEM((tiles, deep, 8 * LANES), bf16),
            pltpu.VMEM((blocks, slots), f32),
            pltpu.VMEM((blocks, slots), i32),
            pltpu.VMEM((blocks, slots), i32),
            pltpu.VMEM((blocks, slots), i32),
            pltpu.VMEM((blocks, slots), i32),
            pltpu.VMEM((8 * deep, wide), bf16),
            pltpu.VMEM((3, deep, wide), f32),
            pltpu.VMEM((deep, wide), f32),
            pltpu.VMEM((4, blocks, slots), f32),
            pltpu.VMEM((tiles, 4, 4, 8, wide), f32),
            pltpu.VMEM((3, blocks, slots), f32),
            pltpu.VMEM((12 * rim, wide), f32),
            pltpu.VMEM((6 * mid, wide), f32),
            pltpu.VMEM((2, 4, rim, LANES), f32),
            pltpu.VMEM((2, 4, rim, LANES), f32),
            pltpu.VMEM((ITERS, 3, 2 * rim, wide), f32),
            pltpu.VMEM((ITERS, 3, 2 * rim, wide), f32),
            pltpu.VMEM((ITERS, 3, mid, wide), f32),
            pltpu.VMEM((ITERS, 3, mid, wide), f32),
            pltpu.VMEM((ITERS, 2, 3, 2 * rim, LANES), f32),
            pltpu.VMEM((ITERS, 2, 3, 2 * rim, LANES), f32),
            dma((2,)),
            dma((2,)),
            dma((ITERS,)),
            dma((ITERS,)),
            dma((ITERS,)),
            dma((ITERS,)),
            dma((ITERS, 2)),
            dma((ITERS, 2)),
        ],
        compiler_params=pltpu.CompilerParams(
            collective_id=0, has_side_effects=True, vmem_limit_bytes=40 * 1024 * 1024
        ),
    )(
        counts,
        v_free.reshape(3, rows, LANES),
        inv_mass.reshape(rows, LANES),
        pairs, angles, bias, friction,
    )
    return velocity.reshape(3, width), impulses


def solution(mesh):
    return jax.shard_map(
        functools.partial(on_device, mesh.shape["grp"]),
        mesh=mesh,
        in_specs=(
            P(None, "grp"),
            P("grp"),
            P(None, ("cell", "grp"), None),
            P(None, ("cell", "grp"), None),
            P(("cell", "grp"), None),
            P(("cell", "grp"), None),
            P(("cell", "grp")),
        ),
        out_specs=(P(None, "grp"), P(None, ("cell", "grp"), None)),
        check_vma=False,
    )
```

profile of v0, /device:TPU:25, one launch (start us, length us, event | category | flops | bytes accessed | tf_op | source)
XLA Modules:
  0.0 36.2 jit_solution(18214164536867927866)
XLA Ops:
  0.6 0.0 copy-start
  0.6 0.0 copy-start.1
  0.7 0.0 copy-start.2
  0.7 0.0 copy-start.3
  0.7 0.0 copy-start.4
  0.7 1.0 %copy.14 = f32[1,3,128,128]{3,2,1,0:T(8,128)S(1)} copy(f32[1,3,128,128]{3,1,2,0:T(4,128)} %bitcast.12) | data formatting | bytes 393216
  1.7 0.0 copy-start.5
  1.7 0.0 copy-done
  1.7 0.0 copy-done.1
  1.7 0.0 copy-done.2
  1.7 0.0 copy-done.3
  1.7 0.0 copy-done.4
  1.8 0.6 %copy-done.5 = s32[32]{0:T(128)S(1)} copy-done((s32[32]{0:T(128)S(1)}, s32[32]{0:T(128)}, u32[]{:S(2)}) %copy-start.5) | copy-done | bytes 152
  2.4 32.3 %shard_map.86 = (f32[3,128,128]{2,1,0:T(8,128)S(1)}, f32[3,32,128]{2,1,0:T(8,128)S(1)}) custom-call(s32[32]{0:T(128)S(1)} %copy-done.5, f32[3,128,128]{2,1,0:T(8,128)S(1)} %bitcast.9, f32[128,128]{1,0:T(8,128)S(1)} %bitcast.11, s32[2,32,128]{2,1,0:T(8,128)S(1)} %copy-done.1, f32[2,32,128]{2,1,0:T(8,128)S(1)} %copy-done.2, f32[32,128]{1,0:T(8,128)S(1)} %copy-done.3, ...), custom_call_target="tpu_custom_call" | custom-call | tf_op jit(solution)/shard_map/pallas_call | solution.py:382
  34.7 0.8 %copy.13 = f32[1,3,128,128]{3,1,2,0:T(4,128)} copy(f32[1,3,128,128]{3,2,1,0:T(8,128)S(1)} %bitcast.10) | data formatting | bytes 393216
  35.5 0.6 %copy.16 = f32[3,32,128]{2,1,0:T(8,128)} copy(f32[3,32,128]{2,1,0:T(8,128)S(1)} %get-tuple-element.9) | data formatting | bytes 98304
Async XLA Ops:
  0.6 1.1 %copy-start = (f32[16384]{0:T(1024)S(1)}, f32[16384]{0:T(1024)}, u32[]{:S(2)}) copy-start(f32[16384]{0:T(1024)} %param.8) | copy-start | bytes 196612
  0.6 1.1 %copy-start.1 = (s32[2,32,128]{2,1,0:T(8,128)S(1)}, s32[2,32,128]{2,1,0:T(8,128)}, u32[]{:S(2)}) copy-start(s32[2,32,128]{2,1,0:T(8,128)} %pairs_ref.1) | copy-start | bytes 98308
  0.7 1.1 %copy-start.2 = (f32[2,32,128]{2,1,0:T(8,128)S(1)}, f32[2,32,128]{2,1,0:T(8,128)}, u32[]{:S(2)}) copy-start(f32[2,32,128]{2,1,0:T(8,128)} %angles_ref.1) | copy-start | bytes 98308
  0.7 1.1 %copy-start.3 = (f32[32,128]{1,0:T(8,128)S(1)}, f32[32,128]{1,0:T(8,128)}, u32[]{:S(2)}) copy-start(f32[32,128]{1,0:T(8,128)} %bias_ref.1) | copy-start | bytes 49156
  0.7 1.1 %copy-start.4 = (f32[32,128]{1,0:T(8,128)S(1)}, f32[32,128]{1,0:T(8,128)}, u32[]{:S(2)}) copy-start(f32[32,128]{1,0:T(8,128)} %friction_ref.1) | copy-start | bytes 49156
  1.7 0.7 %copy-start.5 = (s32[32]{0:T(128)S(1)}, s32[32]{0:T(128)}, u32[]{:S(2)}) copy-start(s32[32]{0:T(128)} %counts_ref.1) | copy-start | bytes 388
where the time goes:
time: 36.8 us; the launch traced here: 36.2 us
  Pallas kernels  32.3 us (88%)
  local copies, waits for them, and re-layouts  3.09 us (8%)
  between operations  0.73 us (2%)
    pallas_call x1, Pallas kernels, on_device(): pl.pallas_call(functools.partial(kernel, cells), out_shape=(jax.ShapeDtyp...  32.3 us
    unnamed x15, local copies, waits for them, and re-layouts  3.09 us

commit v1 on v0

--- a/solution.py
+++ b/solution.py
@@ -25,7 +25,7 @@
     cells,
     counts_ref, v_ref, mass_ref, pairs_ref, angles_ref, bias_ref, friction_ref,
     vel_out, imp_out,
-    hot1, hot2, row1, row2, active,
+    hot1, hot2, spot1, spot2, row1, row2, active,
     h1_ref, h2_ref, l1_ref, l2_ref,
     vb, vfree_all, mass_all, rel, partial, force_ref, acc_outer, acc_inner,
     edge_out, edge_in, outer, outer_in, inner, inner_in, bound_out, bound_in,
@@ -135,6 +135,7 @@
     wide = 2 * LANES
     iota_l = lax.broadcasted_iota(jnp.int32, (wide, wide), 0)
     iota_h = lax.broadcasted_iota(jnp.int32, (half, wide), 0)
+    iota_c = lax.broadcasted_iota(jnp.int32, (LANES, LANES), 1).astype(jnp.float32)
     iota_o = lax.broadcasted_iota(jnp.int32, (rim, wide), 0)
     iota_m = lax.broadcasted_iota(jnp.int32, (mid, wide), 0) + rim
     iota_r = lax.broadcasted_iota(jnp.int32, (rim, wide), 0) + half
@@ -180,6 +181,15 @@
                 if fresh:
                     hot1[i, :, cut] = jnp.where(iota_l == pair_row(l1, u), 1.0, 0.0).astype(jnp.bfloat16)
                     hot2[i, :, cut] = jnp.where(iota_l == pair_row(l2, u), 1.0, 0.0).astype(jnp.bfloat16)
+                    for spot, l in ((spot1, l1), (spot2, l2)):
+                        for s in (2 * u, 2 * u + 1):
+                            lane_row = l[s:s + 1].astype(jnp.float32)
+                            column = jnp.broadcast_to(lane_row, (LANES, LANES)).T
+                            for side in range(2):
+                                found_at = jnp.where(column == iota_c + (side * LANES), 1.0, 0.0)
+                                spot[i, s * LANES:(s + 1) * LANES, side * LANES:(side + 1) * LANES] = (
+                                    found_at.astype(jnp.bfloat16)
+                                )
                     row1[i, :, cut] = jnp.where(iota_h == h1_row, 1.0, 0.0).astype(jnp.bfloat16)
                     row2[i, 0:half, cut] = jnp.where(iota_h == h2_row, 1.0, 0.0).astype(jnp.bfloat16)
                     row2[i, half:deep, cut] = jnp.where(iota_r == h2_row, 1.0, 0.0).astype(jnp.bfloat16)
@@ -215,8 +225,6 @@
             for c in range(count):
                 rel[c, tile_at(i), :] = jnp.concatenate(found[c], axis=0)
 
-    contract = (((1,), (1,)), ((), ()))
-
     def force_terms(i):
         pieces = []
         for c in range(3):
@@ -235,9 +243,7 @@
         return done
 
     def product(weighed, hot):
-        return lax.dot_general(
-            jnp.concatenate(weighed, axis=0), hot, contract, preferred_element_type=jnp.float32
-        )
+        return jnp.dot(jnp.concatenate(weighed, axis=0), hot, preferred_element_type=jnp.float32)
 
     def scatter_outer():
         acc_outer[...] = jnp.zeros(acc_outer.shape, jnp.float32)
@@ -247,15 +253,15 @@
             pieces = force_terms(i)
             mine = weigh(row1[i, 0:rim], pieces, 1)
             theirs = weigh(row2[i, 0:rim], pieces, -1) + weigh(row2[i, half:deep], pieces, -1)
-            acc_outer[0:6 * rim, :] += product(mine, hot1[i])
-            acc_outer[...] += product(theirs, hot2[i])
+            acc_outer[0:6 * rim, :] += product(mine, spot1[i])
+            acc_outer[...] += product(theirs, spot2[i])
 
     def scatter_inner(begin, end):
         @pl.loop(begin, end)
         def _(i):
             pieces = force_terms(i)
-            mine = product(weigh(row1[i, rim:half], pieces, 1), hot1[i])
-            theirs = product(weigh(row2[i, rim:half], pieces, -1), hot2[i])
+            mine = product(weigh(row1[i, rim:half], pieces, 1), spot1[i])
+            theirs = product(weigh(row2[i, rim:half], pieces, -1), spot2[i])
             acc_inner[...] += mine + theirs
 
     lambdas = [jnp.zeros(bias_ref.shape, jnp.float32)] * 3
@@ -390,6 +396,8 @@
         scratch_shapes=[
             pltpu.VMEM((tiles, wide, 8 * LANES), bf16),
             pltpu.VMEM((tiles, wide, 8 * LANES), bf16),
+            pltpu.VMEM((tiles, 8 * LANES, wide), bf16),
+            pltpu.VMEM((tiles, 8 * LANES, wide), bf16),
             pltpu.VMEM((tiles, half, 8 * LANES), bf16),
             pltpu.VMEM((tiles, deep, 8 * LANES), bf16),
             pltpu.VMEM((blocks, slots), f32),

time: 36.8 us -> 35.2 us (0.957)
  Pallas kernels: 32.3 us -> 30.7 us
    pallas_call x1, Pallas kernels: 32.3 us -> 30.7 us  [on_device(): pl.pallas_call(functools.partial(kernel, cells), out_shape=(jax.ShapeDtyp...]
where the time goes in v1:
time: 35.2 us; the launch traced here: 34.5 us
  Pallas kernels  30.7 us (87%)
  local copies, waits for them, and re-layouts  3.09 us (9%)
  between operations  0.73 us (2%)
    pallas_call x1, Pallas kernels, on_device(): pl.pallas_call(functools.partial(kernel, cells), out_shape=(jax.ShapeDtyp...  30.7 us
    unnamed x15, local copies, waits for them, and re-layouts  3.09 us

profile of v1, /device:TPU:25, one launch (start us, length us, event | category | flops | bytes accessed | tf_op | source)
XLA Modules:
  0.0 34.5 jit_solution(12240376297919166719)
XLA Ops:
  0.6 0.0 copy-start
  0.6 0.0 copy-start.1
  0.7 0.0 copy-start.2
  0.7 0.0 copy-start.3
  0.7 0.0 copy-start.4
  0.7 1.0 %copy.14 = f32[1,3,128,128]{3,2,1,0:T(8,128)S(1)} copy(f32[1,3,128,128]{3,1,2,0:T(4,128)} %bitcast.12) | data formatting | bytes 393216
  1.7 0.0 copy-start.5
  1.7 0.0 copy-done
  1.7 0.0 copy-done.1
  1.7 0.0 copy-done.2
  1.7 0.0 copy-done.3
  1.7 0.0 copy-done.4
  1.8 0.6 %copy-done.5 = s32[32]{0:T(128)S(1)} copy-done((s32[32]{0:T(128)S(1)}, s32[32]{0:T(128)}, u32[]{:S(2)}) %copy-start.5) | copy-done | bytes 152
  2.4 30.7 %shard_map.86 = (f32[3,128,128]{2,1,0:T(8,128)S(1)}, f32[3,32,128]{2,1,0:T(8,128)S(1)}) custom-call(s32[32]{0:T(128)S(1)} %copy-done.5, f32[3,128,128]{2,1,0:T(8,128)S(1)} %bitcast.9, f32[128,128]{1,0:T(8,128)S(1)} %bitcast.11, s32[2,32,128]{2,1,0:T(8,128)S(1)} %copy-done.1, f32[2,32,128]{2,1,0:T(8,128)S(1)} %copy-done.2, f32[32,128]{1,0:T(8,128)S(1)} %copy-done.3, ...), custom_call_target="tpu_custom_call" | custom-call | tf_op jit(solution)/shard_map/pallas_call | solution.py:388
  33.1 0.8 %copy.13 = f32[1,3,128,128]{3,1,2,0:T(4,128)} copy(f32[1,3,128,128]{3,2,1,0:T(8,128)S(1)} %bitcast.10) | data formatting | bytes 393216
  33.9 0.6 %copy.16 = f32[3,32,128]{2,1,0:T(8,128)} copy(f32[3,32,128]{2,1,0:T(8,128)S(1)} %get-tuple-element.9) | data formatting | bytes 98304
Async XLA Ops:
  0.6 1.1 %copy-start = (f32[16384]{0:T(1024)S(1)}, f32[16384]{0:T(1024)}, u32[]{:S(2)}) copy-start(f32[16384]{0:T(1024)} %param.8) | copy-start | bytes 196612
  0.6 1.1 %copy-start.1 = (s32[2,32,128]{2,1,0:T(8,128)S(1)}, s32[2,32,128]{2,1,0:T(8,128)}, u32[]{:S(2)}) copy-start(s32[2,32,128]{2,1,0:T(8,128)} %pairs_ref.1) | copy-start | bytes 98308
  0.7 1.1 %copy-start.2 = (f32[2,32,128]{2,1,0:T(8,128)S(1)}, f32[2,32,128]{2,1,0:T(8,128)}, u32[]{:S(2)}) copy-start(f32[2,32,128]{2,1,0:T(8,128)} %angles_ref.1) | copy-start | bytes 98308
  0.7 1.1 %copy-start.3 = (f32[32,128]{1,0:T(8,128)S(1)}, f32[32,128]{1,0:T(8,128)}, u32[]{:S(2)}) copy-start(f32[32,128]{1,0:T(8,128)} %bias_ref.1) | copy-start | bytes 49156
  0.7 1.1 %copy-start.4 = (f32[32,128]{1,0:T(8,128)S(1)}, f32[32,128]{1,0:T(8,128)}, u32[]{:S(2)}) copy-start(f32[32,128]{1,0:T(8,128)} %friction_ref.1) | copy-start | bytes 49156
  1.7 0.7 %copy-start.5 = (s32[32]{0:T(128)S(1)}, s32[32]{0:T(128)}, u32[]{:S(2)}) copy-start(s32[32]{0:T(128)} %counts_ref.1) | copy-start | bytes 388

commit v2 on v1

--- a/solution.py
+++ b/solution.py
@@ -64,16 +64,6 @@
             for sweep in range(ITERS):
                 bound_in[sweep, side] = jnp.zeros(bound_in.shape[2:], jnp.float32)
 
-    between = jnp.logical_and(has_prev, has_next)
-
-    @pl.when(between)
-    def _():
-        pl.semaphore_wait(barrier, 3)
-
-    @pl.when(jnp.logical_not(between))
-    def _():
-        pl.semaphore_wait(barrier, 2)
-
     def edge_copy(side):
         return pltpu.make_async_remote_copy(
             src_ref=edge_out.at[side], dst_ref=edge_in.at[1 - side],
@@ -103,11 +93,6 @@
             send_sem=bound_send.at[sweep, side], recv_sem=bound_recv.at[sweep, 1 - side],
             device_id={"grp": cell + steps[side]}, device_id_type=pl.DeviceIdType.MESH,
         )
-
-    for side in range(2):
-        @pl.when(present[side])
-        def _():
-            edge_copy(side).start()
 
     def place(position):
         own = position - RIM
@@ -135,7 +120,15 @@
     wide = 2 * LANES
     iota_l = lax.broadcasted_iota(jnp.int32, (wide, wide), 0)
     iota_h = lax.broadcasted_iota(jnp.int32, (half, wide), 0)
-    iota_c = lax.broadcasted_iota(jnp.int32, (LANES, LANES), 1).astype(jnp.float32)
+    bf16 = jnp.bfloat16
+    one, zero = jnp.ones((), bf16), jnp.zeros((), bf16)
+    name_l = iota_l.astype(bf16)
+    name_h = lax.broadcasted_iota(jnp.int32, (deep, wide), 0).astype(bf16)
+    name_c = lax.broadcasted_iota(jnp.int32, (LANES, wide), 1).astype(bf16)
+
+    def spread(line, size):
+        return jnp.broadcast_to(line.astype(jnp.float32), (size,) + line.shape[1:]).astype(bf16)
+
     iota_o = lax.broadcasted_iota(jnp.int32, (rim, wide), 0)
     iota_m = lax.broadcasted_iota(jnp.int32, (mid, wide), 0) + rim
     iota_r = lax.broadcasted_iota(jnp.int32, (rim, wide), 0) + half
@@ -153,6 +146,21 @@
 
     vfree_all[:, 0:half] = fold(v_ref[...])
     mass_all[0:half] = fold(mass_ref[...])
+
+    between = jnp.logical_and(has_prev, has_next)
+
+    @pl.when(between)
+    def _():
+        pl.semaphore_wait(barrier, 3)
+
+    @pl.when(jnp.logical_not(between))
+    def _():
+        pl.semaphore_wait(barrier, 2)
+
+    for side in range(2):
+        @pl.when(present[side])
+        def _():
+            edge_copy(side).start()
 
     def tile_at(i):
         return pl.ds(pl.multiple_of(i * 8, 8), 8)
@@ -164,11 +172,15 @@
                 at = base + (t * count + c) * size
                 vb[at:at + size, :] = term
 
-    def picked(g, base, size, c, count, mask):
-        a = base + c * size
-        b = a + count * size
-        block = jnp.where(mask, g[a:a + size] + g[b:b + size], 0.0)
-        return jnp.sum(block.reshape(size // 8, 8, wide), axis=0)
+    def picked(g, base, size, c, count, mask, found=None):
+        terms = []
+        for t in range(2):
+            at = base + (t * count + c) * size
+            held = jnp.zeros((8, wide), jnp.float32) if found is None else found[t]
+            for k in range(0, size, 8):
+                held = jnp.where(mask[k:k + 8], g[at + k:at + k + 8], held)
+            terms.append(held)
+        return terms
 
     def gather_inner(count, fresh):
         @pl.loop(0, tiles)
@@ -179,27 +191,23 @@
                 cut = slice(u * wide, (u + 1) * wide)
                 h1_row, h2_row = pair_row(h1, u), pair_row(h2, u)
                 if fresh:
-                    hot1[i, :, cut] = jnp.where(iota_l == pair_row(l1, u), 1.0, 0.0).astype(jnp.bfloat16)
-                    hot2[i, :, cut] = jnp.where(iota_l == pair_row(l2, u), 1.0, 0.0).astype(jnp.bfloat16)
+                    hot1[i, :, cut] = jnp.where(name_l == spread(pair_row(l1, u), wide), one, zero)
+                    hot2[i, :, cut] = jnp.where(name_l == spread(pair_row(l2, u), wide), one, zero)
                     for spot, l in ((spot1, l1), (spot2, l2)):
                         for s in (2 * u, 2 * u + 1):
                             lane_row = l[s:s + 1].astype(jnp.float32)
-                            column = jnp.broadcast_to(lane_row, (LANES, LANES)).T
-                            for side in range(2):
-                                found_at = jnp.where(column == iota_c + (side * LANES), 1.0, 0.0)
-                                spot[i, s * LANES:(s + 1) * LANES, side * LANES:(side + 1) * LANES] = (
-                                    found_at.astype(jnp.bfloat16)
-                                )
-                    row1[i, :, cut] = jnp.where(iota_h == h1_row, 1.0, 0.0).astype(jnp.bfloat16)
-                    row2[i, 0:half, cut] = jnp.where(iota_h == h2_row, 1.0, 0.0).astype(jnp.bfloat16)
-                    row2[i, half:deep, cut] = jnp.where(iota_r == h2_row, 1.0, 0.0).astype(jnp.bfloat16)
+                            column = jnp.broadcast_to(lane_row, (LANES, LANES)).T.astype(bf16)
+                            column = jnp.concatenate([column, column], axis=1)
+                            spot[i, s * LANES:(s + 1) * LANES, :] = jnp.where(name_c == column, one, zero)
+                    row1[i, :, cut] = jnp.where(name_h[0:half] == spread(h1_row, half), one, zero)
+                    row2[i, :, cut] = jnp.where(name_h == spread(h2_row, deep), one, zero)
                 source = vb[0:2 * count * mid, :]
                 g1 = jnp.dot(source, hot1[i, :, cut], preferred_element_type=jnp.float32)
                 g2 = jnp.dot(source, hot2[i, :, cut], preferred_element_type=jnp.float32)
                 at1, at2 = iota_m == h1_row, iota_m == h2_row
                 for c in range(count):
-                    first = picked(g1, 0, mid, c, count, at1)
-                    second = picked(g2, 0, mid, c, count, at2)
+                    first = sum(picked(g1, 0, mid, c, count, at1))
+                    second = sum(picked(g2, 0, mid, c, count, at2))
                     partial[i, u, c] = first + second if c == 3 else first - second
 
     def gather_outer(count):
@@ -217,8 +225,9 @@
                 g2 = jnp.dot(vb[base:base + 2 * own, :], hot2[i, :, cut], preferred_element_type=jnp.float32)
                 at1, at2, at_rim = iota_o == h1_row, iota_o == h2_row, iota_r == h2_row
                 for c in range(count):
-                    first = picked(g1, 0, rim, c, count, at1)
-                    second = picked(g2, 0, rim, c, count, at2) + picked(g2, own, rim, c, count, at_rim)
+                    first = sum(picked(g1, 0, rim, c, count, at1))
+                    second = picked(g2, 0, rim, c, count, at2)
+                    second = sum(picked(g2, own, rim, c, count, at_rim, second))
                     both_ends = partial[i, u, c] + (first + second if c == 3 else first - second)
                     line = jnp.sum(both_ends, axis=0, keepdims=True)
                     found[c] += [line[:, 0:LANES], line[:, LANES:wide]]
@@ -302,6 +311,7 @@
                 force = force + second_tan[c] * lambdas[2]
             force_ref[c] = force
 
+        early = max(1, tiles // 4 if last else tiles // 2)
         scatter_outer()
         for c in range(3):
             for part in range(2):
@@ -310,7 +320,7 @@
                 outer[sweep, c, part * rim:(part + 1) * rim] = acc_outer[a:a + rim, :] + acc_outer[b:b + rim, :]
         outer_copy(sweep).start()
         acc_inner[...] = jnp.zeros(acc_inner.shape, jnp.float32)
-        scatter_inner(0, tiles // 2)
+        scatter_inner(0, early)
         outer_copy(sweep).wait_recv()
         for side in range(2):
             cut = slice(side * LANES, (side + 1) * LANES)
@@ -320,7 +330,7 @@
             @pl.when(present[side])
             def _():
                 bound_copy(sweep, side).start()
-        scatter_inner(tiles // 2, tiles)
+        scatter_inner(early, tiles)
         for c in range(3):
             a = c * mid
             b = a + 3 * mid

time: 35.2 us -> 35.1 us (level); the launches traced: 34.5 us -> 35 us
  Pallas kernels: 30.7 us -> 31.1 us
    pallas_call x1, Pallas kernels: 30.7 us -> 31.1 us  [on_device(): pl.pallas_call(functools.partial(kernel, cells), out_shape=(jax.ShapeDtyp...]
where the time goes in v2:
time: 35.1 us; the launch traced here: 35 us
  Pallas kernels  31.1 us (89%)
  local copies, waits for them, and re-layouts  3.09 us (9%)
  between operations  0.73 us (2%)
    pallas_call x1, Pallas kernels, on_device(): pl.pallas_call(functools.partial(kernel, cells), out_shape=(jax.ShapeDtyp...  31.1 us
    unnamed x15, local copies, waits for them, and re-layouts  3.09 us

profile of v2, /device:TPU:25, one launch (start us, length us, event | category | flops | bytes accessed | tf_op | source)
XLA Modules:
  0.0 35.0 jit_solution(10522926509944869151)
XLA Ops:
  0.6 0.0 copy-start
  0.6 0.0 copy-start.1
  0.7 0.0 copy-start.2
  0.7 0.0 copy-start.3
  0.7 0.0 copy-start.4
  0.7 1.0 %copy.14 = f32[1,3,128,128]{3,2,1,0:T(8,128)S(1)} copy(f32[1,3,128,128]{3,1,2,0:T(4,128)} %bitcast.12) | data formatting | bytes 393216
  1.7 0.0 copy-start.5
  1.7 0.0 copy-done
  1.7 0.0 copy-done.1
  1.7 0.0 copy-done.2
  1.7 0.0 copy-done.3
  1.7 0.0 copy-done.4
  1.8 0.6 %copy-done.5 = s32[32]{0:T(128)S(1)} copy-done((s32[32]{0:T(128)S(1)}, s32[32]{0:T(128)}, u32[]{:S(2)}) %copy-start.5) | copy-done | bytes 152
  2.4 31.1 %shard_map.86 = (f32[3,128,128]{2,1,0:T(8,128)S(1)}, f32[3,32,128]{2,1,0:T(8,128)S(1)}) custom-call(s32[32]{0:T(128)S(1)} %copy-done.5, f32[3,128,128]{2,1,0:T(8,128)S(1)} %bitcast.9, f32[128,128]{1,0:T(8,128)S(1)} %bitcast.11, s32[2,32,128]{2,1,0:T(8,128)S(1)} %copy-done.1, f32[2,32,128]{2,1,0:T(8,128)S(1)} %copy-done.2, f32[32,128]{1,0:T(8,128)S(1)} %copy-done.3, ...), custom_call_target="tpu_custom_call" | custom-call | tf_op jit(solution)/shard_map/pallas_call | solution.py:398
  33.5 0.8 %copy.13 = f32[1,3,128,128]{3,1,2,0:T(4,128)} copy(f32[1,3,128,128]{3,2,1,0:T(8,128)S(1)} %bitcast.10) | data formatting | bytes 393216
  34.3 0.6 %copy.16 = f32[3,32,128]{2,1,0:T(8,128)} copy(f32[3,32,128]{2,1,0:T(8,128)S(1)} %get-tuple-element.9) | data formatting | bytes 98304
Async XLA Ops:
  0.6 1.1 %copy-start = (f32[16384]{0:T(1024)S(1)}, f32[16384]{0:T(1024)}, u32[]{:S(2)}) copy-start(f32[16384]{0:T(1024)} %param.8) | copy-start | bytes 196612
  0.6 1.1 %copy-start.1 = (s32[2,32,128]{2,1,0:T(8,128)S(1)}, s32[2,32,128]{2,1,0:T(8,128)}, u32[]{:S(2)}) copy-start(s32[2,32,128]{2,1,0:T(8,128)} %pairs_ref.1) | copy-start | bytes 98308
  0.7 1.1 %copy-start.2 = (f32[2,32,128]{2,1,0:T(8,128)S(1)}, f32[2,32,128]{2,1,0:T(8,128)}, u32[]{:S(2)}) copy-start(f32[2,32,128]{2,1,0:T(8,128)} %angles_ref.1) | copy-start | bytes 98308
  0.7 1.1 %copy-start.3 = (f32[32,128]{1,0:T(8,128)S(1)}, f32[32,128]{1,0:T(8,128)}, u32[]{:S(2)}) copy-start(f32[32,128]{1,0:T(8,128)} %bias_ref.1) | copy-start | bytes 49156
  0.7 1.1 %copy-start.4 = (f32[32,128]{1,0:T(8,128)S(1)}, f32[32,128]{1,0:T(8,128)}, u32[]{:S(2)}) copy-start(f32[32,128]{1,0:T(8,128)} %friction_ref.1) | copy-start | bytes 49156
  1.7 0.7 %copy-start.5 = (s32[32]{0:T(128)S(1)}, s32[32]{0:T(128)}, u32[]{:S(2)}) copy-start(s32[32]{0:T(128)} %counts_ref.1) | copy-start | bytes 388

commit v3 on v2

--- a/solution.py
+++ b/solution.py
@@ -31,7 +31,7 @@
     edge_out, edge_in, outer, outer_in, inner, inner_in, bound_out, bound_in,
     edge_send, edge_recv, outer_send, outer_recv, inner_send, inner_recv, bound_send, bound_recv,
 ):
-    rows = v_ref.shape[1]
+    rows = v_ref.shape[1] // LANES
     rim = RIM // LANES
     half = rows // 2
     deep = half + rim
@@ -53,9 +53,10 @@
                 barrier, inc=1, device_id={"grp": cell + steps[side]}, device_id_type=pl.DeviceIdType.MESH
             )
 
-    edge_out[0, 0:3] = v_ref[:, 0:rim]
+    free = v_ref[...].reshape(3, rows, LANES)
+    edge_out[0, 0:3] = free[:, 0:rim]
     edge_out[0, 3] = mass_ref[0:rim]
-    edge_out[1, 0:3] = v_ref[:, rows - rim:rows]
+    edge_out[1, 0:3] = free[:, rows - rim:rows]
     edge_out[1, 3] = mass_ref[rows - rim:rows]
     for side in range(2):
         @pl.when(jnp.logical_not(present[side]))
@@ -117,7 +118,11 @@
     def pair_row(tile, u):
         return jnp.concatenate([tile[2 * u:2 * u + 1], tile[2 * u + 1:2 * u + 2]], axis=1)
 
+    def quad_row(tile, u):
+        return jnp.concatenate([tile[4 * u + n:4 * u + n + 1] for n in range(4)], axis=1)
+
     wide = 2 * LANES
+    broad = 4 * LANES
     iota_l = lax.broadcasted_iota(jnp.int32, (wide, wide), 0)
     iota_h = lax.broadcasted_iota(jnp.int32, (half, wide), 0)
     bf16 = jnp.bfloat16
@@ -129,9 +134,9 @@
     def spread(line, size):
         return jnp.broadcast_to(line.astype(jnp.float32), (size,) + line.shape[1:]).astype(bf16)
 
-    iota_o = lax.broadcasted_iota(jnp.int32, (rim, wide), 0)
-    iota_m = lax.broadcasted_iota(jnp.int32, (mid, wide), 0) + rim
-    iota_r = lax.broadcasted_iota(jnp.int32, (rim, wide), 0) + half
+    iota_o = lax.broadcasted_iota(jnp.int32, (rim, broad), 0)
+    iota_m = lax.broadcasted_iota(jnp.int32, (mid, broad), 0) + rim
+    iota_r = lax.broadcasted_iota(jnp.int32, (rim, broad), 0) + half
 
     sin_p, cos_p = jnp.sin(angles_ref[0]), jnp.cos(angles_ref[0])
     sin_q, cos_q = jnp.sin(angles_ref[1]), jnp.cos(angles_ref[1])
@@ -144,7 +149,7 @@
         upper = jnp.concatenate([block[..., rows - rim:rows, :], block[..., half:rows - rim, :]], axis=-2)
         return jnp.concatenate([lower, upper], axis=-1)
 
-    vfree_all[:, 0:half] = fold(v_ref[...])
+    vfree_all[:, 0:half] = fold(free)
     mass_all[0:half] = fold(mass_ref[...])
 
     between = jnp.logical_and(has_prev, has_next)
@@ -176,7 +181,7 @@
         terms = []
         for t in range(2):
             at = base + (t * count + c) * size
-            held = jnp.zeros((8, wide), jnp.float32) if found is None else found[t]
+            held = jnp.zeros((8, broad), jnp.float32) if found is None else found[t]
             for k in range(0, size, 8):
                 held = jnp.where(mask[k:k + 8], g[at + k:at + k + 8], held)
             terms.append(held)
@@ -201,10 +206,12 @@
                             spot[i, s * LANES:(s + 1) * LANES, :] = jnp.where(name_c == column, one, zero)
                     row1[i, :, cut] = jnp.where(name_h[0:half] == spread(h1_row, half), one, zero)
                     row2[i, :, cut] = jnp.where(name_h == spread(h2_row, deep), one, zero)
-                source = vb[0:2 * count * mid, :]
+            source = vb[0:2 * count * mid, :]
+            for u in range(2):
+                cut = slice(u * broad, (u + 1) * broad)
                 g1 = jnp.dot(source, hot1[i, :, cut], preferred_element_type=jnp.float32)
                 g2 = jnp.dot(source, hot2[i, :, cut], preferred_element_type=jnp.float32)
-                at1, at2 = iota_m == h1_row, iota_m == h2_row
+                at1, at2 = iota_m == quad_row(h1, u), iota_m == quad_row(h2, u)
                 for c in range(count):
                     first = sum(picked(g1, 0, mid, c, count, at1))
                     second = sum(picked(g2, 0, mid, c, count, at2))
@@ -218,9 +225,9 @@
         def _(i):
             h1, h2 = h1_ref[tile_at(i), :], h2_ref[tile_at(i), :]
             found = [[] for _ in range(count)]
-            for u in range(4):
-                cut = slice(u * wide, (u + 1) * wide)
-                h1_row, h2_row = pair_row(h1, u), pair_row(h2, u)
+            for u in range(2):
+                cut = slice(u * broad, (u + 1) * broad)
+                h1_row, h2_row = quad_row(h1, u), quad_row(h2, u)
                 g1 = jnp.dot(vb[base:base + own, :], hot1[i, :, cut], preferred_element_type=jnp.float32)
                 g2 = jnp.dot(vb[base:base + 2 * own, :], hot2[i, :, cut], preferred_element_type=jnp.float32)
                 at1, at2, at_rim = iota_o == h1_row, iota_o == h2_row, iota_r == h2_row
@@ -230,7 +237,7 @@
                     second = sum(picked(g2, own, rim, c, count, at_rim, second))
                     both_ends = partial[i, u, c] + (first + second if c == 3 else first - second)
                     line = jnp.sum(both_ends, axis=0, keepdims=True)
-                    found[c] += [line[:, 0:LANES], line[:, LANES:wide]]
+                    found[c] += [line[:, n * LANES:(n + 1) * LANES] for n in range(4)]
             for c in range(count):
                 rel[c, tile_at(i), :] = jnp.concatenate(found[c], axis=0)
 
@@ -419,7 +426,7 @@
             pltpu.VMEM((3, deep, wide), f32),
             pltpu.VMEM((deep, wide), f32),
             pltpu.VMEM((4, blocks, slots), f32),
-            pltpu.VMEM((tiles, 4, 4, 8, wide), f32),
+            pltpu.VMEM((tiles, 2, 4, 8, 2 * wide), f32),
             pltpu.VMEM((3, blocks, slots), f32),
             pltpu.VMEM((12 * rim, wide), f32),
             pltpu.VMEM((6 * mid, wide), f32),
@@ -445,7 +452,7 @@
         ),
     )(
         counts,
-        v_free.reshape(3, rows, LANES),
+        v_free,
         inv_mass.reshape(rows, LANES),
         pairs, angles, bias, friction,
     )

time: 35.1 us -> 39.2 us (1.12)
  local copies, waits for them, and re-layouts: 3.09 us -> 6.84 us
    unnamed x15 -> x16, local copies, waits for them, and re-layouts: 3.09 us -> 6.84 us
where the time goes in v3:
time: 39.2 us; the launch traced here: 38.7 us
  Pallas kernels  31.2 us (80%)
  local copies, waits for them, and re-layouts  6.84 us (17%)
  between operations  0.66 us (2%)
    pallas_call x1, Pallas kernels, on_device(): pl.pallas_call(functools.partial(kernel, cells), out_shape=(jax.ShapeDtyp...  31.2 us
    unnamed x16, local copies, waits for them, and re-layouts  6.84 us

profile of v3, /device:TPU:25, one launch (start us, length us, event | category | flops | bytes accessed | tf_op | source)
XLA Modules:
  0.0 38.7 jit_solution(11276211810599513991)
XLA Ops:
  0.6 0.0 copy-start.6
  0.6 0.6 %copy-done.6 = s32[32]{0:T(128)S(1)} copy-done((s32[32]{0:T(128)S(1)}, s32[32]{0:T(128)}, u32[]{:S(2)}) %copy-start.6) | copy-done | bytes 152
  1.3 0.0 copy-start
  1.3 0.9 %copy-done = f32[3,16384]{1,0:T(4,128)S(1)} copy-done((f32[3,16384]{1,0:T(4,128)S(1)}, f32[3,16384]{1,0:T(4,128)}, u32[]{:S(2)}) %copy-start) | copy-done | bytes 196632
  2.2 0.0 copy-start.1
  2.2 0.8 %copy-done.1 = f32[16384]{0:T(1024)S(1)} copy-done((f32[16384]{0:T(1024)S(1)}, f32[16384]{0:T(1024)}, u32[]{:S(2)}) %copy-start.1) | copy-done | bytes 65560
  3.1 0.0 copy-start.2
  3.1 0.8 %copy-done.2 = s32[2,32,128]{2,1,0:T(8,128)S(1)} copy-done((s32[2,32,128]{2,1,0:T(8,128)S(1)}, s32[2,32,128]{2,1,0:T(8,128)}, u32[]{:S(2)}) %copy-start.2) | copy-done | bytes 32792
  3.8 0.0 copy-start.3
  3.8 0.8 %copy-done.3 = f32[2,32,128]{2,1,0:T(8,128)S(1)} copy-done((f32[2,32,128]{2,1,0:T(8,128)S(1)}, f32[2,32,128]{2,1,0:T(8,128)}, u32[]{:S(2)}) %copy-start.3) | copy-done | bytes 32792
  4.6 0.0 copy-start.4
  4.6 0.7 %copy-done.4 = f32[32,128]{1,0:T(8,128)S(1)} copy-done((f32[32,128]{1,0:T(8,128)S(1)}, f32[32,128]{1,0:T(8,128)}, u32[]{:S(2)}) %copy-start.4) | copy-done | bytes 16408
  5.3 0.0 copy-start.5
  5.3 0.7 %copy-done.5 = f32[32,128]{1,0:T(8,128)S(1)} copy-done((f32[32,128]{1,0:T(8,128)S(1)}, f32[32,128]{1,0:T(8,128)}, u32[]{:S(2)}) %copy-start.5) | copy-done | bytes 16408
  6.0 31.2 %shard_map.86 = (f32[3,128,128]{2,1,0:T(8,128)S(1)}, f32[3,32,128]{2,1,0:T(8,128)S(1)}) custom-call(s32[32]{0:T(128)S(1)} %copy-done.6, f32[3,16384]{1,0:T(4,128)S(1)} %copy-done, f32[128,128]{1,0:T(8,128)S(1)} %bitcast.6, s32[2,32,128]{2,1,0:T(8,128)S(1)} %copy-done.2, f32[2,32,128]{2,1,0:T(8,128)S(1)} %copy-done.3, f32[32,128]{1,0:T(8,128)S(1)} %copy-done.4, ...), custom_call_target="tpu_custom_call" | custom-call | tf_op jit(solution)/shard_map/pallas_call | solution.py:405
  37.3 0.8 %copy.11 = f32[1,3,128,128]{3,1,2,0:T(4,128)} copy(f32[1,3,128,128]{3,2,1,0:T(8,128)S(1)} %bitcast.5) | data formatting | bytes 393216
  38.1 0.6 %copy.13 = f32[3,32,128]{2,1,0:T(8,128)} copy(f32[3,32,128]{2,1,0:T(8,128)S(1)} %get-tuple-element.9) | data formatting | bytes 98304
Async XLA Ops:
  0.6 0.7 %copy-start.6 = (s32[32]{0:T(128)S(1)}, s32[32]{0:T(128)}, u32[]{:S(2)}) copy-start(s32[32]{0:T(128)} %counts_ref.1) | copy-start | bytes 388
  1.3 0.9 %copy-start = (f32[3,16384]{1,0:T(4,128)S(1)}, f32[3,16384]{1,0:T(4,128)}, u32[]{:S(2)}) copy-start(f32[3,16384]{1,0:T(4,128)} %v_ref.1) | copy-start | bytes 589828
  2.2 0.8 %copy-start.1 = (f32[16384]{0:T(1024)S(1)}, f32[16384]{0:T(1024)}, u32[]{:S(2)}) copy-start(f32[16384]{0:T(1024)} %param.8) | copy-start | bytes 196612
  3.1 0.8 %copy-start.2 = (s32[2,32,128]{2,1,0:T(8,128)S(1)}, s32[2,32,128]{2,1,0:T(8,128)}, u32[]{:S(2)}) copy-start(s32[2,32,128]{2,1,0:T(8,128)} %pairs_ref.1) | copy-start | bytes 98308
  3.8 0.8 %copy-start.3 = (f32[2,32,128]{2,1,0:T(8,128)S(1)}, f32[2,32,128]{2,1,0:T(8,128)}, u32[]{:S(2)}) copy-start(f32[2,32,128]{2,1,0:T(8,128)} %angles_ref.1) | copy-start | bytes 98308
  4.6 0.7 %copy-start.4 = (f32[32,128]{1,0:T(8,128)S(1)}, f32[32,128]{1,0:T(8,128)}, u32[]{:S(2)}) copy-start(f32[32,128]{1,0:T(8,128)} %bias_ref.1) | copy-start | bytes 49156
  5.3 0.7 %copy-start.5 = (f32[32,128]{1,0:T(8,128)S(1)}, f32[32,128]{1,0:T(8,128)}, u32[]{:S(2)}) copy-start(f32[32,128]{1,0:T(8,128)} %friction_ref.1) | copy-start | bytes 49156

commit v4 on v3

--- a/solution.py
+++ b/solution.py
@@ -23,8 +23,9 @@
 
 def kernel(
     cells,
-    counts_ref, v_ref, mass_ref, pairs_ref, angles_ref, bias_ref, friction_ref,
-    vel_out, imp_out,
+    counts_ref, v_hbm, mass_hbm, pairs_hbm, angles_hbm, bias_hbm, friction_hbm,
+    vel_hbm, imp_hbm,
+    vel_out, imp_out, store_sems, v_ref, mass_ref, pairs_ref, angles_ref, bias_ref, friction_ref, load_sems,
     hot1, hot2, spot1, spot2, row1, row2, active,
     h1_ref, h2_ref, l1_ref, l2_ref,
     vb, vfree_all, mass_all, rel, partial, force_ref, acc_outer, acc_inner,
@@ -52,6 +53,29 @@
             pl.semaphore_signal(
                 barrier, inc=1, device_id={"grp": cell + steps[side]}, device_id_type=pl.DeviceIdType.MESH
             )
+
+    loads = [
+        pltpu.make_async_copy(source, target, load_sems.at[n])
+        for n, (source, target) in enumerate((
+            (pairs_hbm, pairs_ref), (v_hbm, v_ref), (mass_hbm, mass_ref),
+            (angles_hbm, angles_ref), (bias_hbm, bias_ref), (friction_hbm, friction_ref),
+        ))
+    ]
+    stores = [
+        pltpu.make_async_copy(imp_out, imp_hbm, store_sems.at[0]),
+        pltpu.make_async_copy(
+            vel_out.at[:, pl.ds(rim, rows - 2 * rim)], vel_hbm.at[:, pl.ds(rim, rows - 2 * rim)], store_sems.at[1]
+        ),
+    ] + [
+        pltpu.make_async_copy(
+            vel_out.at[:, pl.ds(start, rim)], vel_hbm.at[:, pl.ds(start, rim)], store_sems.at[2 + side]
+        )
+        for side, start in enumerate((0, rows - rim))
+    ]
+    for load in loads:
+        load.start()
+    for load in loads:
+        load.wait()
 
     free = v_ref[...].reshape(3, rows, LANES)
     edge_out[0, 0:3] = free[:, 0:rim]
@@ -318,7 +342,7 @@
                 force = force + second_tan[c] * lambdas[2]
             force_ref[c] = force
 
-        early = max(1, tiles // 4 if last else tiles // 2)
+        early = max(1, tiles // 4)
         scatter_outer()
         for c in range(3):
             for part in range(2):
@@ -353,6 +377,8 @@
                 vel_out[c, rim:half] = speeds[c][:, 0:LANES]
                 vel_out[c, half:rows - rim] = speeds[c][:, LANES:wide]
                 imp_out[c] = lambdas[c]
+            stores[0].start()
+            stores[1].start()
         else:
             store_terms(speeds, 0)
             gather_inner(3, False)
@@ -378,6 +404,8 @@
                 store_terms(speeds, 6 * mid + 6 * rim * part)
         if not last:
             gather_outer(3)
+    stores[2].start()
+    stores[3].start()
     for side in range(2):
         @pl.when(present[side])
         def _():
@@ -387,6 +415,8 @@
     for sweep in range(ITERS):
         outer_copy(sweep).wait_send()
         inner_copy(sweep).wait_send()
+    for store in stores:
+        store.wait()
 
 
 def on_device(cells, v_free, inv_mass, pairs, angles, bias, friction, counts):
@@ -400,7 +430,6 @@
     tiles = blocks // 8
     wide = 2 * LANES
     f32, bf16, i32 = jnp.float32, jnp.bfloat16, jnp.int32
-    vmem = pl.BlockSpec(memory_space=pltpu.VMEM)
     dma = pltpu.SemaphoreType.DMA
     velocity, impulses = pl.pallas_call(
         functools.partial(kernel, cells),
@@ -408,9 +437,19 @@
             jax.ShapeDtypeStruct((3, rows, LANES), f32),
             jax.ShapeDtypeStruct((3, blocks, slots), f32),
         ),
-        in_specs=[pl.BlockSpec(memory_space=pltpu.SMEM)] + [vmem] * 6,
-        out_specs=(vmem, vmem),
+        in_specs=[pl.BlockSpec(memory_space=pltpu.SMEM)] + [pl.BlockSpec(memory_space=pl.ANY)] * 6,
+        out_specs=(pl.BlockSpec(memory_space=pl.ANY),) * 2,
         scratch_shapes=[
+            pltpu.VMEM((3, rows, LANES), f32),
+            pltpu.VMEM((3, blocks, slots), f32),
+            dma((4,)),
+            pltpu.VMEM((3, width), f32),
+            pltpu.VMEM((rows, LANES), f32),
+            pltpu.VMEM((2, blocks, slots), i32),
+            pltpu.VMEM((2, blocks, slots), f32),
+            pltpu.VMEM((blocks, slots), f32),
+            pltpu.VMEM((blocks, slots), f32),
+            dma((6,)),
             pltpu.VMEM((tiles, wide, 8 * LANES), bf16),
             pltpu.VMEM((tiles, wide, 8 * LANES), bf16),
             pltpu.VMEM((tiles, 8 * LANES, wide), bf16),
@@ -448,7 +487,7 @@
             dma((ITERS, 2)),
         ],
         compiler_params=pltpu.CompilerParams(
-            collective_id=0, has_side_effects=True, vmem_limit_bytes=40 * 1024 * 1024
+            collective_id=0, has_side_effects=True, vmem_limit_bytes=56 * 1024 * 1024
         ),
     )(
         counts,

time: 39.2 us -> 35.8 us (0.913)
  local copies, waits for them, and re-layouts: 6.84 us -> 2.4 us
  Pallas kernels: 31.2 us -> 32.6 us
    unnamed x16 -> x4, local copies, waits for them, and re-layouts: 6.84 us -> 2.4 us
    pallas_call x1, Pallas kernels: 31.2 us -> 32.6 us  [on_device(): pl.pallas_call(functools.partial(kernel, cells), out_shape=(jax.ShapeDtyp...]
where the time goes in v4:
time: 35.8 us; the launch traced here: 35.6 us
  Pallas kernels  32.6 us (91%)
  local copies, waits for them, and re-layouts  2.4 us (7%)
  between operations  0.65 us (2%)
    pallas_call x1, Pallas kernels, on_device(): pl.pallas_call(functools.partial(kernel, cells), out_shape=(jax.ShapeDtyp...  32.6 us
    unnamed x4, local copies, waits for them, and re-layouts  2.4 us

profile of v4, /device:TPU:25, one launch (start us, length us, event | category | flops | bytes accessed | tf_op | source)
XLA Modules:
  0.0 35.6 jit_solution(9344761535911378680)
XLA Ops:
  0.6 32.6 %shard_map.86 = (f32[3,128,128]{2,1,0:T(8,128)}, f32[3,32,128]{2,1,0:T(8,128)}) custom-call(s32[32]{0:T(128)} %counts_ref.1, f32[3,16384]{1,0:T(4,128)} %v_hbm.1, f32[128,128]{1,0:T(8,128)} %bitcast.7, s32[2,32,128]{2,1,0:T(8,128)} %pairs_hbm.1, f32[2,32,128]{2,1,0:T(8,128)} %angles_hbm.1, f32[32,128]{1,0:T(8,128)} %bias_hbm.1, f32[32,128]{1,0:T(8,128)} %friction_hbm.1), custom_call_target="tpu_custom_call" | custom-call | tf_op jit(solution)/shard_map/pallas_call | solution.py:434
  33.2 0.0 copy-start
  33.2 1.8 %copy.11 = f32[1,3,128,128]{3,1,2,0:T(4,128)} copy(f32[1,3,128,128]{3,2,1,0:T(8,128)} %bitcast.6) | data formatting | bytes 393216
  35.0 0.0 copy-done
  35.0 0.6 %copy.13 = f32[3,32,128]{2,1,0:T(8,128)} copy(f32[3,32,128]{2,1,0:T(8,128)S(1)} %copy-done) | data formatting | bytes 98304
Async XLA Ops:
  33.2 1.8 %copy-start = (f32[3,32,128]{2,1,0:T(8,128)S(1)}, f32[3,32,128]{2,1,0:T(8,128)}, u32[]{:S(2)}) copy-start(f32[3,32,128]{2,1,0:T(8,128)} %get-tuple-element.9) | copy-start | bytes 147460
